TPU v7x, 32 devices: a whole 2x2x4 slice. The times are simulated.
32 devices in a mesh: groups: 2 (over x), rows: 16 (over z, y, core).
Axes of the slice: x: 2, y: 2, z: 4, core: 2. Of those that a mesh axis runs over, the one named last changes fastest.
Arguments:
- genotypes: bfloat16 [32768, 4096], P(('groups', 'rows')), parts along dimension 0, may hold values from -6 to 6
- sample_factors: float32 [32768, 64], P(('groups', 'rows')), parts along dimension 0, may hold values from -2.1213203 to 2.1213203
- snp_factors: float32 [20480, 64], P(('groups', 'rows')), parts along dimension 0, may hold values from -2.1213203 to 2.1213203
- coverage: int32 [32, 64], P('groups'), parts along dimension 0, may hold values from 0 to 159, as said below
Outputs:
- new_samples: float32 [32768, 64], P(('groups', 'rows')), parts along dimension 0
- new_snps: float32 [20480, 64], P(('groups', 'rows')), parts along dimension 0
There are 2 independent parts, one for each index of `groups`. A program takes and returns all parts, laid end to end along the dimension named above; each array names one. Nothing has to cross between parts.
Inputs may be any that keep to these rules, and one draw needn't show every extreme that they name: `coverage`: each row lists 64 distinct SNP blocks in ascending order, exactly 4 of them among blocks o * 10 to (o + 1) * 10 - 1 for every o; every SNP block is listed by at least one batch.
All inputs are finite; a program needn't handle non-finite values.
Results may differ from a plain program's by a relative error of at most 0.0067.
Values may be sent and summed in bfloat16 or wider, within the bound.
A program may use at most 128 MiB of HBM per device.

v0:
```python
import math
import jax
import jax.numpy as jnp
from jax import lax
from jax.sharding import PartitionSpec as P

ROUNDS = 2
weight_decay = 0.02


def on_device(genotypes, sample_factors, snp_factors, coverage):
    devices = lax.axis_size("rows")
    position = lax.axis_index("rows")
    samples_here = genotypes.shape[0]
    rank_width = sample_factors.shape[1]
    covered = coverage.shape[1]
    tile_size = genotypes.shape[1] // covered
    per_owner = covered // devices
    own_blocks = snp_factors.shape[0] // tile_size
    own_list = lax.dynamic_index_in_dim(coverage, position, 0, keepdims=False)
    local_list = (
        lax.dynamic_slice_in_dim(coverage, position * per_owner, per_owner, 1)
        - position * own_blocks
    )
    one_hot = (
        local_list[:, :, None] == jnp.arange(own_blocks, dtype=jnp.int32)[None, None, :]
    ).astype(jnp.float32)
    observers = jnp.sum(one_hot, axis=(0, 1))
    snp_step = 0.5 * math.sqrt(rank_width) / (samples_here * observers)
    sample_step = 0.5 * math.sqrt(rank_width) / (covered * tile_size)
    samples = sample_factors
    snps = snp_factors
    for iteration in range(ROUNDS):
        snp_bf16 = snps.astype(jnp.bfloat16).reshape(own_blocks, tile_size, rank_width)
        gathered = lax.all_gather(snp_bf16, "rows", axis=0, tiled=True)
        panels = gathered[own_list].reshape(covered * tile_size, rank_width)
        predicted = lax.dot_general(
            samples.astype(jnp.bfloat16),
            panels,
            (((1,), (1,)), ((), ())),
            preferred_element_type=jnp.float32,
        )
        residual = (genotypes.astype(jnp.float32) - predicted).astype(jnp.bfloat16)
        gradient = jnp.dot(residual, panels, preferred_element_type=jnp.float32)
        samples = (1.0 - weight_decay) * samples + sample_step * gradient
        sample_bf16 = samples.astype(jnp.bfloat16)
        predicted = lax.dot_general(
            sample_bf16, panels, (((1,), (1,)), ((), ())), preferred_element_type=jnp.float32
        )
        residual = (genotypes.astype(jnp.float32) - predicted).astype(jnp.bfloat16)
        snp_gradient = lax.dot_general(
            residual, sample_bf16, (((0,), (0,)), ((), ())), preferred_element_type=jnp.float32
        )
        incoming_terms = lax.all_to_all(
            snp_gradient.reshape(devices, per_owner, tile_size, rank_width).astype(jnp.bfloat16),
            "rows",
            split_axis=0,
            concat_axis=0,
            tiled=True,
        ).astype(jnp.float32)
        summed = jnp.einsum(
            "bpk,bptr->ktr", one_hot, incoming_terms, precision=lax.Precision.HIGHEST
        )
        snps = (1.0 - weight_decay) * snps + (snp_step[:, None, None] * summed).reshape(
            own_blocks * tile_size, rank_width
        )
    return (samples, snps)


def solution(mesh):
    placed = (
        P(("groups", "rows"), None),
        P(("groups", "rows"), None),
        P(("groups", "rows"), None),
        P("groups", None),
    )
    return jax.shard_map(
        on_device,
        mesh=mesh,
        in_specs=placed,
        out_specs=(P(("groups", "rows"), None), P(("groups", "rows"), None)),
        check_vma=False,
    )
```

profile of v0, /device:TPU:0, one launch (start us, length us, event | category | flops | bytes accessed | tf_op | source)
XLA Modules:
  0.0 190.6 jit_solution(12273409029608411657)
XLA Ops:
  7.2 1.1 copy.32
  8.3 0.7 convert_element_type.52
  9.0 12.1 %copy.31 = bf16[1024,4096]{0,1:T(8,128)(2,1)} copy(bf16[1024,4096]{1,0:T(8,128)(2,1)} %param.4) | data formatting | bytes 16777216 | tf_op args[0]
  21.1 35.6 %all-gather.3.cloned.1.call-done = bf16[160,64,64]{2,1,0:T(8,128)(2,1)} async-done(((bf16[10,64,64]{2,1,0:T(8,128)(2,1)}), bf16[160,64,64]{2,1,0:T(8,128)(2,1)}) %all-gather.3.cloned.1.call-update) | async-done | bytes 1310736 | tf_op jit(solution)/shard_map/all_gather | solution.py:35
  56.8 2.5 %gather_fusion = bf16[64,64,64]{2,1,0:T(8,128)(2,1)S(1)} fusion(bf16[160,64,64]{2,1,0:T(8,128)(2,1)} %all-gather.3.cloned.1.call-done, s32[1024]{0:T(1024)S(1)} %pad_clamp_fusion), kind=kCustom, calls=%fused_computation | custom fusion | bytes 1048832 | tf_op jit(solution)/shard_map/gather | solution.py:36
  59.3 7.2 %fusion.11 = f32[1024,64]{0,1:T(8,128)S(1)} fusion(bf16[4096,64]{1,0:T(8,128)(2,1)S(1)} %bitcast.58, bf16[1024,4096]{0,1:T(8,128)(2,1)} %copy.31, f32[1024,64]{0,1:T(8,128)S(1)} %copy-done.1), kind=kOutput, calls=%fused_computation.21 | convolution fusion | flops 1086586880 | bytes 9437184 | tf_op jit(solution)/shard_map/dot_general | solution.py:44
  66.5 8.1 %convolution_convert_fusion.1 = bf16[4096,64]{0,1:T(8,128)(2,1)S(1)} fusion(bf16[1024,4096]{0,1:T(8,128)(2,1)} %copy.31, bf16[4096,64]{1,0:T(8,128)(2,1)S(1)} %bitcast.59, f32[1024,64]{0,1:T(8,128)S(1)} %fusion.11), kind=kOutput, calls=%fused_computation.11 | convolution fusion | flops 1086717952 | bytes 9699328 | tf_op jit(solution)/shard_map/dot_general | solution.py:51
  74.6 1.1 convert_element_type.59
  75.7 1.9 copy.36
  77.6 1.5 reshape.84
  79.2 3.6 %all-to-all-start = ((bf16[16,2,8192]{2,1,0:T(2,128)(2,1)}), bf16[16,2,8192]{2,1,0:T(2,128)(2,1)S(1)}, u32[]{:S(2)}, u32[]{:S(2)}) async-start(bf16[16,2,8192]{2,1,0:T(2,128)(2,1)} %reshape.84), calls=%async_computation | async-start | bytes 1048576 | tf_op jit(solution)/shard_map/all_to_all | solution.py:54
  82.8 0.2 all-gather.5.cloned.1.call-start
  83.0 0.1 constant_dynamic-slice_fusion
  83.1 0.1 copy.50
  83.2 0.1 convert_reduce_fusion
  83.3 13.9 %all-to-all-done = bf16[16,2,8192]{2,1,0:T(2,128)(2,1)S(1)} async-done(((bf16[16,2,8192]{2,1,0:T(2,128)(2,1)}), bf16[16,2,8192]{2,1,0:T(2,128)(2,1)S(1)}, u32[]{:S(2)}, u32[]{:S(2)}) %all-to-all-start) | async-done | bytes 524320 | tf_op jit(solution)/shard_map/all_to_all | solution.py:54
  97.2 0.7 reshape.85
  97.9 0.7 fusion.7
  98.6 0.1 copy.38
  98.7 0.7 fusion.18
  99.4 42.7 %all-gather.5.cloned.1.call-done = bf16[160,64,64]{2,1,0:T(8,128)(2,1)} async-done(((bf16[10,64,64]{2,1,0:T(8,128)(2,1)}), bf16[160,64,64]{2,1,0:T(8,128)(2,1)}) %all-gather.5.cloned.1.call-update) | async-done | bytes 1310736 | tf_op jit(solution)/shard_map/all_gather | solution.py:35
  142.1 2.5 %gather_fusion.1 = bf16[64,64,64]{2,1,0:T(8,128)(2,1)S(1)} fusion(bf16[160,64,64]{2,1,0:T(8,128)(2,1)} %all-gather.5.cloned.1.call-done, s32[1024]{0:T(1024)S(1)} %pad_clamp_fusion), kind=kCustom, calls=%fused_computation.1 | custom fusion | bytes 1048832 | tf_op jit(solution)/shard_map/gather | solution.py:36
  144.6 7.1 %fusion.10 = f32[1024,64]{0,1:T(8,128)S(1)} fusion(bf16[4096,64]{1,0:T(8,128)(2,1)S(1)} %bitcast.56, bf16[1024,4096]{0,1:T(8,128)(2,1)} %copy.31, f32[1024,64]{0,1:T(8,128)S(1)} %fusion.11), kind=kOutput, calls=%fused_computation.20 | convolution fusion | flops 1086586880 | bytes 9437184 | tf_op jit(solution)/shard_map/dot_general | solution.py:44
  151.7 8.2 %convolution_convert_fusion = bf16[4096,64]{0,1:T(8,128)(2,1)S(1)} fusion(bf16[1024,4096]{0,1:T(8,128)(2,1)} %copy.31, bf16[4096,64]{1,0:T(8,128)(2,1)S(1)} %bitcast.57, f32[1024,64]{0,1:T(8,128)S(1)} %fusion.10), kind=kOutput, calls=%fused_computation.10 | convolution fusion | flops 1086717952 | bytes 9699328 | tf_op jit(solution)/shard_map/dot_general | solution.py:51
  160.0 1.1 convert_element_type.65
  161.1 1.9 copy.41
  163.0 0.7 reshape.86
  163.7 17.6 %all_to_all.10 = bf16[16,2,8192]{2,1,0:T(2,128)(2,1)S(1)} all-to-all(bf16[16,2,8192]{2,1,0:T(2,128)(2,1)S(1)} %reshape.86), channel_id=1, replica_groups=mesh['groups'=2,'rows'=16] {'rows'}, dimensions={0} | all-to-all | bytes 1048576 | tf_op jit(solution)/shard_map/all_to_all | solution.py:54
  181.4 0.7 reshape.87
  182.0 0.7 fusion.6
  182.7 0.1 copy.43
  182.9 0.8 copy.44
  (14 shorter events, 0.2 us)
Async XLA Ops:
  7.2 49.6 %all-gather.3.cloned.1.call-start = ((), (), s32[]{:S(2)}) async-start(), calls=%async_computation.2 | async-start | bytes 2785280 | tf_op jit(solution)/shard_map/all_gather | solution.py:35
  9.0 12.1 %copy-start = (s32[16,64]{1,0:T(8,128)S(1)}, s32[16,64]{1,0:T(8,128)}, u32[]{:S(2)}) copy-start(s32[16,64]{1,0:T(8,128)} %param.7) | copy-start | bytes 12292
  9.0 50.3 %copy-start.1 = (f32[1024,64]{0,1:T(8,128)S(1)}, f32[1024,64]{0,1:T(8,128)}, u32[]{:S(2)}) copy-start(f32[1024,64]{0,1:T(8,128)} %param.5) | copy-start | bytes 786436
  79.2 18.0 %all-to-all-start = ((bf16[16,2,8192]{2,1,0:T(2,128)(2,1)}), bf16[16,2,8192]{2,1,0:T(2,128)(2,1)S(1)}, u32[]{:S(2)}, u32[]{:S(2)}) async-start(bf16[16,2,8192]{2,1,0:T(2,128)(2,1)} %reshape.84), calls=%async_computation | async-start | bytes 1048576 | tf_op jit(solution)/shard_map/all_to_all | solution.py:54
  82.8 59.3 %all-gather.5.cloned.1.call-start = ((), (), s32[]{:S(2)}) async-start(), calls=%async_computation.3 | async-start | bytes 2785280 | tf_op jit(solution)/shard_map/all_gather | solution.py:35
  151.7 12.0 %copy-start.2 = (f32[1024,64]{0,1:T(8,128)}, f32[1024,64]{0,1:T(8,128)S(1)}, u32[]{:S(2)}) copy-start(f32[1024,64]{0,1:T(8,128)S(1)} %fusion.10) | copy-start | bytes 786436
Sparse Core Ops, SparseCore 0:
  10.9 45.8 all-gather.2
  99.5 42.4 all-gather.4
where the time goes:
time: 191 us
  waiting for transfers between devices  92.2 us (48%)
  matrix products  32.1 us (17%)
  local copies, waits for them, and re-layouts  29 us (15%)
  blocking collectives  17.6 us (9%)
  between operations  14.2 us (7%)
  starting transfers between devices  3.83 us (2%)
    all_gather x2, waiting for transfers between devices, on_device(): gathered = lax.all_gather(snp_bf16, 'rows', axis=0, tiled=True)  78.3 us
    unnamed x14, local copies, waits for them, and re-layouts  17.6 us
    all_to_all x1, blocking collectives, on_device(): lax.all_to_all(snp_gradient.reshape(devices, per_owner, tile_size, rank_w...  17.6 us
    dot_general x2, matrix products, on_device(): lax.dot_general(residual, sample_bf16, (((0,), (0,)), ((), ())), preferre...  16.4 us
    dot_general x2, matrix products, on_device(): gradient = jnp.dot(residual, panels, preferred_element_type=jnp.float32)  14.3 us
    all_to_all x1, waiting for transfers between devices, on_device(): lax.all_to_all(snp_gradient.reshape(devices, per_owner, tile_size, rank_w...  13.9 us
    convert_element_type x4, local copies, waits for them, and re-layouts, on_device(): snp_gradient.reshape(devices, per_owner, tile_size, rank_width)  6.07 us
    gather x2, local copies, waits for them, and re-layouts, on_device(): panels = gathered[own_list].reshape(covered * tile_size, rank_width)  4.97 us
  transfers between devices with their start and end apart: 3, of which 3 were waited for; matrix products, arithmetic and copies ran while one was open for 7% of the time, Pallas kernels for 0%

commit v1 on v0

--- a/solution.py
+++ b/solution.py
@@ -1,3 +1,4 @@
+import functools
 import math
 import jax
 import jax.numpy as jnp
@@ -6,6 +7,39 @@
 
 ROUNDS = 2
 weight_decay = 0.02
+
+
+def try_all_ladders_up(v0, row_axis):
+    mixed_arr = lax.axis_index(row_axis)
+    plain = lax.axis_size(row_axis)
+    work_now, before, outer = (plain, mixed_arr, v0.shape[0])
+    z1 = x_new = v0
+    block_out = lax.dynamic_update_slice_in_dim(
+        jnp.zeros(
+            tuple((ii * work_now if k0 == 0 else ii for k0, ii in enumerate(v0.shape))), v0.dtype
+        ),
+        v0,
+        before * outer,
+        axis=0,
+    )
+    for to_i in range(1, work_now // 2 + 1):
+        z1 = lax.ppermute(
+            z1, row_axis, perm=tuple(((k0, (k0 + 1) % work_now) for k0 in range(work_now)))
+        )
+        block_out = lax.dynamic_update_slice_in_dim(
+            block_out, z1, (before - to_i) % work_now * outer, axis=0
+        )
+        if 2 * to_i < work_now:
+            x_new = lax.ppermute(
+                x_new, row_axis, perm=tuple(((k0, (k0 - 1) % work_now) for k0 in range(work_now)))
+            )
+            block_out = lax.dynamic_update_slice_in_dim(
+                block_out, x_new, (before + to_i) % work_now * outer, axis=0
+            )
+    return block_out
+
+
+_finish_patch = functools.partial(try_all_ladders_up, row_axis="rows")
 
 
 def on_device(genotypes, sample_factors, snp_factors, coverage):
@@ -32,7 +66,7 @@
     snps = snp_factors
     for iteration in range(ROUNDS):
         snp_bf16 = snps.astype(jnp.bfloat16).reshape(own_blocks, tile_size, rank_width)
-        gathered = lax.all_gather(snp_bf16, "rows", axis=0, tiled=True)
+        gathered = _finish_patch(snp_bf16)
         panels = gathered[own_list].reshape(covered * tile_size, rank_width)
         predicted = lax.dot_general(
             samples.astype(jnp.bfloat16),

time: 191 us -> 217 us (1.14)
  starting transfers between devices: 3.83 us -> 68 us
  waiting for transfers between devices: 92.2 us -> 66.3 us
  between operations: 14.2 us -> 1.16 us
    all_gather x2 -> x0, waiting for transfers between devices: 78.3 us -> none  [on_device(): gathered = lax.all_gather(snp_bf16, 'rows', axis=0, tiled=True)]
    ppermute x0 -> x30, starting transfers between devices: none -> 64.5 us  [the longest x14 63.8 us: try_all_ladders_up(): lax.ppermute(x_new, row_axis, perm=tuple(((k0, (k0 - 1) % work_now) for k...]
    ppermute x0 -> x30, waiting for transfers between devices: none -> 52.2 us  [the longest x16 52.1 us: try_all_ladders_up(): lax.ppermute(z1, row_axis, perm=tuple(((k0, (k0 + 1) % work_now) for k0 i...]
    unnamed x14 -> x20, local copies, waits for them, and re-layouts: 17.6 us -> 18.3 us
  transfers between devices with their start and end apart: 3 -> 31, of which waited for: 3 -> 16; matrix products, arithmetic and copies ran while one was open for 7% -> 7% of each run, Pallas kernels for 0% -> 0%
where the time goes in v1:
time: 217 us
  starting transfers between devices  68 us (31%)
  waiting for transfers between devices  66.3 us (31%)
  matrix products  33.8 us (16%)
  local copies, waits for them, and re-layouts  30.1 us (14%)
  blocking collectives  17.1 us (8%)
    ppermute x14, starting transfers between devices, try_all_ladders_up(): lax.ppermute(x_new, row_axis, perm=tuple(((k0, (k0 - 1) % work_now) for k...  63.8 us
    ppermute x16, waiting for transfers between devices, try_all_ladders_up(): lax.ppermute(z1, row_axis, perm=tuple(((k0, (k0 + 1) % work_now) for k0 i...  52.1 us
    unnamed x20, local copies, waits for them, and re-layouts  18.3 us
    all_to_all x1, blocking collectives, on_device(): lax.all_to_all(snp_gradient.reshape(devices, per_owner, tile_size, rank_w...  17.1 us
    dot_general x2, matrix products, on_device(): lax.dot_general(residual, sample_bf16, (((0,), (0,)), ((), ())), preferre...  16.4 us
    dot_general x2, matrix products, on_device(): gradient = jnp.dot(residual, panels, preferred_element_type=jnp.float32)  16 us
    all_to_all x1, waiting for transfers between devices, on_device(): lax.all_to_all(snp_gradient.reshape(devices, per_owner, tile_size, rank_w...  14.1 us
    convert_element_type x4, local copies, waits for them, and re-layouts, on_device(): snp_gradient.reshape(devices, per_owner, tile_size, rank_width)  6.06 us
  transfers between devices with their start and end apart: 31, of which 16 were waited for; matrix products, arithmetic and copies ran while one was open for 7% of the time, Pallas kernels for 0%

profile of v1, /device:TPU:0, one launch (start us, length us, event | category | flops | bytes accessed | tf_op | source)
XLA Modules:
  0.0 216.8 jit_solution(9825041600872774595)
XLA Ops:
  2.2 5.1 %collective-permute-start.1 = (bf16[10,64,64]{2,1,0:T(8,128)(2,1)S(1)}, bf16[10,64,64]{2,1,0:T(8,128)(2,1)S(1)}, u32[]{:S(2)}, u32[]{:S(2)}) collective-permute-start(bf16[10,64,64]{2,1,0:T(8,128)(2,1)S(1)} %bitcast.63), channel_id=1, source_target_pairs={{0,15},{1,0},{2,1},{3,2},{4,3},{5,4},{6,5},{7,6},{8,7},{9,8},{10,9... | collective-permute-start | bytes 245768 | tf_op jit(solution)/shard_map/ppermute | solution.py:33
  7.3 12.0 %copy.31 = bf16[1024,4096]{0,1:T(8,128)(2,1)} copy(bf16[1024,4096]{1,0:T(8,128)(2,1)} %param.4) | data formatting | bytes 16777216 | tf_op args[0]
  20.2 4.4 %collective-permute-start.3 = (bf16[10,64,64]{2,1,0:T(8,128)(2,1)S(1)}, bf16[10,64,64]{2,1,0:T(8,128)(2,1)S(1)}, u32[]{:S(2)}, u32[]{:S(2)}) collective-permute-start(bf16[10,64,64]{2,1,0:T(8,128)(2,1)S(1)} %collective-permute-done.1), channel_id=1, source_target_pairs={{0,15},{1,0},{2,1},{3,2},{4,3},{5,4},{6,5},{7,6},{8,7},{9,8},{10,9... | collective-permute-start | bytes 245768 | tf_op jit(solution)/shard_map/ppermute | solution.py:33
  24.7 2.9 %collective-permute-done.2 = bf16[10,64,64]{2,1,0:T(8,128)(2,1)S(1)} collective-permute-done((bf16[10,64,64]{2,1,0:T(8,128)(2,1)S(1)}, bf16[10,64,64]{2,1,0:T(8,128)(2,1)S(1)}, u32[]{:S(2)}, u32[]{:S(2)}) %collective-permute-start.2) | collective-permute-done | bytes 81952 | tf_op jit(solution)/shard_map/ppermute | solution.py:26
  27.6 4.5 %collective-permute-start.5 = (bf16[10,64,64]{2,1,0:T(8,128)(2,1)S(1)}, bf16[10,64,64]{2,1,0:T(8,128)(2,1)S(1)}, u32[]{:S(2)}, u32[]{:S(2)}) collective-permute-start(bf16[10,64,64]{2,1,0:T(8,128)(2,1)S(1)} %collective-permute-done.3), channel_id=1, source_target_pairs={{0,15},{1,0},{2,1},{3,2},{4,3},{5,4},{6,5},{7,6},{8,7},{9,8},{10,9... | collective-permute-start | bytes 245768 | tf_op jit(solution)/shard_map/ppermute | solution.py:33
  32.2 2.9 %collective-permute-done.4 = bf16[10,64,64]{2,1,0:T(8,128)(2,1)S(1)} collective-permute-done((bf16[10,64,64]{2,1,0:T(8,128)(2,1)S(1)}, bf16[10,64,64]{2,1,0:T(8,128)(2,1)S(1)}, u32[]{:S(2)}, u32[]{:S(2)}) %collective-permute-start.4) | collective-permute-done | bytes 81952 | tf_op jit(solution)/shard_map/ppermute | solution.py:26
  35.2 4.4 %collective-permute-start.7 = (bf16[10,64,64]{2,1,0:T(8,128)(2,1)S(1)}, bf16[10,64,64]{2,1,0:T(8,128)(2,1)S(1)}, u32[]{:S(2)}, u32[]{:S(2)}) collective-permute-start(bf16[10,64,64]{2,1,0:T(8,128)(2,1)S(1)} %collective-permute-done.5), channel_id=1, source_target_pairs={{0,15},{1,0},{2,1},{3,2},{4,3},{5,4},{6,5},{7,6},{8,7},{9,8},{10,9... | collective-permute-start | bytes 245768 | tf_op jit(solution)/shard_map/ppermute | solution.py:33
  39.7 3.0 %collective-permute-done.6 = bf16[10,64,64]{2,1,0:T(8,128)(2,1)S(1)} collective-permute-done((bf16[10,64,64]{2,1,0:T(8,128)(2,1)S(1)}, bf16[10,64,64]{2,1,0:T(8,128)(2,1)S(1)}, u32[]{:S(2)}, u32[]{:S(2)}) %collective-permute-start.6) | collective-permute-done | bytes 81952 | tf_op jit(solution)/shard_map/ppermute | solution.py:26
  42.7 4.4 %collective-permute-start.9 = (bf16[10,64,64]{2,1,0:T(8,128)(2,1)S(1)}, bf16[10,64,64]{2,1,0:T(8,128)(2,1)S(1)}, u32[]{:S(2)}, u32[]{:S(2)}) collective-permute-start(bf16[10,64,64]{2,1,0:T(8,128)(2,1)S(1)} %collective-permute-done.7), channel_id=1, source_target_pairs={{0,15},{1,0},{2,1},{3,2},{4,3},{5,4},{6,5},{7,6},{8,7},{9,8},{10,9... | collective-permute-start | bytes 245768 | tf_op jit(solution)/shard_map/ppermute | solution.py:33
  47.2 3.0 %collective-permute-done.8 = bf16[10,64,64]{2,1,0:T(8,128)(2,1)S(1)} collective-permute-done((bf16[10,64,64]{2,1,0:T(8,128)(2,1)S(1)}, bf16[10,64,64]{2,1,0:T(8,128)(2,1)S(1)}, u32[]{:S(2)}, u32[]{:S(2)}) %collective-permute-start.8) | collective-permute-done | bytes 81952 | tf_op jit(solution)/shard_map/ppermute | solution.py:26
  50.3 4.4 %collective-permute-start.11 = (bf16[10,64,64]{2,1,0:T(8,128)(2,1)S(1)}, bf16[10,64,64]{2,1,0:T(8,128)(2,1)S(1)}, u32[]{:S(2)}, u32[]{:S(2)}) collective-permute-start(bf16[10,64,64]{2,1,0:T(8,128)(2,1)S(1)} %collective-permute-done.9), channel_id=1, source_target_pairs={{0,15},{1,0},{2,1},{3,2},{4,3},{5,4},{6,5},{7,6},{8,7},{9,8},{10,9... | collective-permute-start | bytes 245768 | tf_op jit(solution)/shard_map/ppermute | solution.py:33
  54.8 3.0 %collective-permute-done.10 = bf16[10,64,64]{2,1,0:T(8,128)(2,1)S(1)} collective-permute-done((bf16[10,64,64]{2,1,0:T(8,128)(2,1)S(1)}, bf16[10,64,64]{2,1,0:T(8,128)(2,1)S(1)}, u32[]{:S(2)}, u32[]{:S(2)}) %collective-permute-start.10) | collective-permute-done | bytes 81952 | tf_op jit(solution)/shard_map/ppermute | solution.py:26
  57.8 4.4 %collective-permute-start.13 = (bf16[10,64,64]{2,1,0:T(8,128)(2,1)S(1)}, bf16[10,64,64]{2,1,0:T(8,128)(2,1)S(1)}, u32[]{:S(2)}, u32[]{:S(2)}) collective-permute-start(bf16[10,64,64]{2,1,0:T(8,128)(2,1)S(1)} %collective-permute-done.11), channel_id=1, source_target_pairs={{0,15},{1,0},{2,1},{3,2},{4,3},{5,4},{6,5},{7,6},{8,7},{9,8},{10,9... | collective-permute-start | bytes 245768 | tf_op jit(solution)/shard_map/ppermute | solution.py:33
  62.3 2.9 %collective-permute-done.12 = bf16[10,64,64]{2,1,0:T(8,128)(2,1)S(1)} collective-permute-done((bf16[10,64,64]{2,1,0:T(8,128)(2,1)S(1)}, bf16[10,64,64]{2,1,0:T(8,128)(2,1)S(1)}, u32[]{:S(2)}, u32[]{:S(2)}) %collective-permute-start.12) | collective-permute-done | bytes 81952 | tf_op jit(solution)/shard_map/ppermute | solution.py:26
  65.3 7.4 %collective-permute-done.14 = bf16[10,64,64]{2,1,0:T(8,128)(2,1)S(1)} collective-permute-done((bf16[10,64,64]{2,1,0:T(8,128)(2,1)S(1)}, bf16[10,64,64]{2,1,0:T(8,128)(2,1)S(1)}, u32[]{:S(2)}, u32[]{:S(2)}) %collective-permute-start.14) | collective-permute-done | bytes 81952 | tf_op jit(solution)/shard_map/ppermute | solution.py:26
  74.4 7.9 %fusion.11 = f32[1024,64]{0,1:T(8,128)S(1)} fusion(bf16[4096,64]{1,0:T(8,128)(2,1)} %bitcast.60, bf16[1024,4096]{0,1:T(8,128)(2,1)} %copy.31, f32[1024,64]{0,1:T(8,128)S(1)} %copy-done.3), kind=kOutput, calls=%fused_computation.21 | convolution fusion | flops 1086586880 | bytes 9437184 | tf_op jit(solution)/shard_map/dot_general | solution.py:78
  83.0 8.1 %convolution_convert_fusion.1 = bf16[4096,64]{0,1:T(8,128)(2,1)S(1)} fusion(bf16[1024,4096]{0,1:T(8,128)(2,1)} %copy.31, bf16[4096,64]{1,0:T(8,128)(2,1)S(1)} %bitcast.61, f32[1024,64]{0,1:T(8,128)S(1)} %fusion.11), kind=kOutput, calls=%fused_computation.11 | convolution fusion | flops 1086717952 | bytes 9699328 | tf_op jit(solution)/shard_map/dot_general | solution.py:85
  95.8 3.6 %all-to-all-start = ((bf16[16,2,8192]{2,1,0:T(2,128)(2,1)}), bf16[16,2,8192]{2,1,0:T(2,128)(2,1)S(1)}, u32[]{:S(2)}, u32[]{:S(2)}) async-start(bf16[16,2,8192]{2,1,0:T(2,128)(2,1)} %reshape.84), calls=%async_computation | async-start | bytes 1048576 | tf_op jit(solution)/shard_map/all_to_all | solution.py:88
  99.7 14.1 %all-to-all-done = bf16[16,2,8192]{2,1,0:T(2,128)(2,1)S(1)} async-done(((bf16[16,2,8192]{2,1,0:T(2,128)(2,1)}), bf16[16,2,8192]{2,1,0:T(2,128)(2,1)S(1)}, u32[]{:S(2)}, u32[]{:S(2)}) %all-to-all-start) | async-done | bytes 524320 | tf_op jit(solution)/shard_map/all_to_all | solution.py:88
  115.4 4.4 %collective-permute-start.16 = (bf16[10,64,64]{2,1,0:T(8,128)(2,1)S(1)}, bf16[10,64,64]{2,1,0:T(8,128)(2,1)S(1)}, u32[]{:S(2)}, u32[]{:S(2)}) collective-permute-start(bf16[10,64,64]{2,1,0:T(8,128)(2,1)S(1)} %bitcast.66), channel_id=1, source_target_pairs={{0,15},{1,0},{2,1},{3,2},{4,3},{5,4},{6,5},{7,6},{8,7},{9,8},{10,9... | collective-permute-start | bytes 245768 | tf_op jit(solution)/shard_map/ppermute | solution.py:33
  122.9 4.5 %collective-permute-start.18 = (bf16[10,64,64]{2,1,0:T(8,128)(2,1)S(1)}, bf16[10,64,64]{2,1,0:T(8,128)(2,1)S(1)}, u32[]{:S(2)}, u32[]{:S(2)}) collective-permute-start(bf16[10,64,64]{2,1,0:T(8,128)(2,1)S(1)} %collective-permute-done.16), channel_id=1, source_target_pairs={{0,15},{1,0},{2,1},{3,2},{4,3},{5,4},{6,5},{7,6},{8,7},{9,8},{10,9... | collective-permute-start | bytes 245768 | tf_op jit(solution)/shard_map/ppermute | solution.py:33
  127.4 3.0 %collective-permute-done.17 = bf16[10,64,64]{2,1,0:T(8,128)(2,1)S(1)} collective-permute-done((bf16[10,64,64]{2,1,0:T(8,128)(2,1)S(1)}, bf16[10,64,64]{2,1,0:T(8,128)(2,1)S(1)}, u32[]{:S(2)}, u32[]{:S(2)}) %collective-permute-start.17) | collective-permute-done | bytes 81952 | tf_op jit(solution)/shard_map/ppermute | solution.py:26
  130.4 4.7 %collective-permute-start.20 = (bf16[10,64,64]{2,1,0:T(8,128)(2,1)S(1)}, bf16[10,64,64]{2,1,0:T(8,128)(2,1)S(1)}, u32[]{:S(2)}, u32[]{:S(2)}) collective-permute-start(bf16[10,64,64]{2,1,0:T(8,128)(2,1)S(1)} %collective-permute-done.18), channel_id=1, source_target_pairs={{0,15},{1,0},{2,1},{3,2},{4,3},{5,4},{6,5},{7,6},{8,7},{9,8},{10,9... | collective-permute-start | bytes 245768 | tf_op jit(solution)/shard_map/ppermute | solution.py:33
  137.9 4.6 %collective-permute-start.22 = (bf16[10,64,64]{2,1,0:T(8,128)(2,1)S(1)}, bf16[10,64,64]{2,1,0:T(8,128)(2,1)S(1)}, u32[]{:S(2)}, u32[]{:S(2)}) collective-permute-start(bf16[10,64,64]{2,1,0:T(8,128)(2,1)S(1)} %collective-permute-done.20), channel_id=1, source_target_pairs={{0,15},{1,0},{2,1},{3,2},{4,3},{5,4},{6,5},{7,6},{8,7},{9,8},{10,9... | collective-permute-start | bytes 245768 | tf_op jit(solution)/shard_map/ppermute | solution.py:33
  145.5 4.6 %collective-permute-start.24 = (bf16[10,64,64]{2,1,0:T(8,128)(2,1)S(1)}, bf16[10,64,64]{2,1,0:T(8,128)(2,1)S(1)}, u32[]{:S(2)}, u32[]{:S(2)}) collective-permute-start(bf16[10,64,64]{2,1,0:T(8,128)(2,1)S(1)} %collective-permute-done.22), channel_id=1, source_target_pairs={{0,15},{1,0},{2,1},{3,2},{4,3},{5,4},{6,5},{7,6},{8,7},{9,8},{10,9... | collective-permute-start | bytes 245768 | tf_op jit(solution)/shard_map/ppermute | solution.py:33
  153.0 4.6 %collective-permute-start.26 = (bf16[10,64,64]{2,1,0:T(8,128)(2,1)S(1)}, bf16[10,64,64]{2,1,0:T(8,128)(2,1)S(1)}, u32[]{:S(2)}, u32[]{:S(2)}) collective-permute-start(bf16[10,64,64]{2,1,0:T(8,128)(2,1)S(1)} %collective-permute-done.24), channel_id=1, source_target_pairs={{0,15},{1,0},{2,1},{3,2},{4,3},{5,4},{6,5},{7,6},{8,7},{9,8},{10,9... | collective-permute-start | bytes 245768 | tf_op jit(solution)/shard_map/ppermute | solution.py:33
  157.7 2.9 %collective-permute-done.25 = bf16[10,64,64]{2,1,0:T(8,128)(2,1)S(1)} collective-permute-done((bf16[10,64,64]{2,1,0:T(8,128)(2,1)S(1)}, bf16[10,64,64]{2,1,0:T(8,128)(2,1)S(1)}, u32[]{:S(2)}, u32[]{:S(2)}) %collective-permute-start.25) | collective-permute-done | bytes 81952 | tf_op jit(solution)/shard_map/ppermute | solution.py:26
  160.6 4.6 %collective-permute-start.28 = (bf16[10,64,64]{2,1,0:T(8,128)(2,1)S(1)}, bf16[10,64,64]{2,1,0:T(8,128)(2,1)S(1)}, u32[]{:S(2)}, u32[]{:S(2)}) collective-permute-start(bf16[10,64,64]{2,1,0:T(8,128)(2,1)S(1)} %collective-permute-done.26), channel_id=1, source_target_pairs={{0,15},{1,0},{2,1},{3,2},{4,3},{5,4},{6,5},{7,6},{8,7},{9,8},{10,9... | collective-permute-start | bytes 245768 | tf_op jit(solution)/shard_map/ppermute | solution.py:33
  168.1 7.4 %collective-permute-done.29 = bf16[10,64,64]{2,1,0:T(8,128)(2,1)S(1)} collective-permute-done((bf16[10,64,64]{2,1,0:T(8,128)(2,1)S(1)}, bf16[10,64,64]{2,1,0:T(8,128)(2,1)S(1)}, u32[]{:S(2)}, u32[]{:S(2)}) %collective-permute-start.29) | collective-permute-done | bytes 81952 | tf_op jit(solution)/shard_map/ppermute | solution.py:26
  177.2 8.2 %fusion.10 = f32[1024,64]{0,1:T(8,128)S(1)} fusion(bf16[4096,64]{1,0:T(8,128)(2,1)} %bitcast.58, bf16[1024,4096]{0,1:T(8,128)(2,1)} %copy.31, f32[1024,64]{0,1:T(8,128)} %copy-done.5), kind=kOutput, calls=%fused_computation.20 | convolution fusion | flops 1086586880 | bytes 9437184 | tf_op jit(solution)/shard_map/dot_general | solution.py:78
  185.4 8.2 %convolution_convert_fusion = bf16[4096,64]{0,1:T(8,128)(2,1)S(1)} fusion(bf16[1024,4096]{0,1:T(8,128)(2,1)} %copy.31, bf16[4096,64]{1,0:T(8,128)(2,1)S(1)} %bitcast.59, f32[1024,64]{0,1:T(8,128)S(1)} %fusion.10), kind=kOutput, calls=%fused_computation.10 | convolution fusion | flops 1086717952 | bytes 9699328 | tf_op jit(solution)/shard_map/dot_general | solution.py:85
  197.4 17.1 %all_to_all.10 = bf16[16,2,8192]{2,1,0:T(2,128)(2,1)S(1)} all-to-all(bf16[16,2,8192]{2,1,0:T(2,128)(2,1)S(1)} %reshape.86), channel_id=1, replica_groups=mesh['groups'=2,'rows'=16] {'rows'}, dimensions={0} | all-to-all | bytes 1048576 | tf_op jit(solution)/shard_map/all_to_all | solution.py:88
  (108 shorter events, 34.1 us)
Async XLA Ops:
  1.7 18.4 %collective-permute-start = (bf16[10,64,64]{2,1,0:T(8,128)(2,1)S(1)}, bf16[10,64,64]{2,1,0:T(8,128)(2,1)S(1)}, u32[]{:S(2)}, u32[]{:S(2)}) collective-permute-start(bf16[10,64,64]{2,1,0:T(8,128)(2,1)S(1)} %bitcast.62), channel_id=1, source_target_pairs={{0,1},{1,2},{2,3},{3,4},{4,5},{5,6},{6,7},{7,8},{8,9},{9,10},{10,1... | collective-permute-start | bytes 245768 | tf_op jit(solution)/shard_map/ppermute | solution.py:26
  2.2 17.9 %collective-permute-start.1 = (bf16[10,64,64]{2,1,0:T(8,128)(2,1)S(1)}, bf16[10,64,64]{2,1,0:T(8,128)(2,1)S(1)}, u32[]{:S(2)}, u32[]{:S(2)}) collective-permute-start(bf16[10,64,64]{2,1,0:T(8,128)(2,1)S(1)} %bitcast.63), channel_id=1, source_target_pairs={{0,15},{1,0},{2,1},{3,2},{4,3},{5,4},{6,5},{7,6},{8,7},{9,8},{10,9... | collective-permute-start | bytes 245768 | tf_op jit(solution)/shard_map/ppermute | solution.py:33
  20.1 7.5 %collective-permute-start.2 = (bf16[10,64,64]{2,1,0:T(8,128)(2,1)S(1)}, bf16[10,64,64]{2,1,0:T(8,128)(2,1)S(1)}, u32[]{:S(2)}, u32[]{:S(2)}) collective-permute-start(bf16[10,64,64]{2,1,0:T(8,128)(2,1)S(1)} %collective-permute-done), channel_id=1, source_target_pairs={{0,1},{1,2},{2,3},{3,4},{4,5},{5,6},{6,7},{7,8},{8,9},{9,10},{10,1... | collective-permute-start | bytes 245768 | tf_op jit(solution)/shard_map/ppermute | solution.py:26
  20.2 7.4 %collective-permute-start.3 = (bf16[10,64,64]{2,1,0:T(8,128)(2,1)S(1)}, bf16[10,64,64]{2,1,0:T(8,128)(2,1)S(1)}, u32[]{:S(2)}, u32[]{:S(2)}) collective-permute-start(bf16[10,64,64]{2,1,0:T(8,128)(2,1)S(1)} %collective-permute-done.1), channel_id=1, source_target_pairs={{0,15},{1,0},{2,1},{3,2},{4,3},{5,4},{6,5},{7,6},{8,7},{9,8},{10,9... | collective-permute-start | bytes 245768 | tf_op jit(solution)/shard_map/ppermute | solution.py:33
  27.6 7.5 %collective-permute-start.4 = (bf16[10,64,64]{2,1,0:T(8,128)(2,1)S(1)}, bf16[10,64,64]{2,1,0:T(8,128)(2,1)S(1)}, u32[]{:S(2)}, u32[]{:S(2)}) collective-permute-start(bf16[10,64,64]{2,1,0:T(8,128)(2,1)S(1)} %collective-permute-done.2), channel_id=1, source_target_pairs={{0,1},{1,2},{2,3},{3,4},{4,5},{5,6},{6,7},{7,8},{8,9},{9,10},{10,1... | collective-permute-start | bytes 245768 | tf_op jit(solution)/shard_map/ppermute | solution.py:26
  27.6 7.5 %collective-permute-start.5 = (bf16[10,64,64]{2,1,0:T(8,128)(2,1)S(1)}, bf16[10,64,64]{2,1,0:T(8,128)(2,1)S(1)}, u32[]{:S(2)}, u32[]{:S(2)}) collective-permute-start(bf16[10,64,64]{2,1,0:T(8,128)(2,1)S(1)} %collective-permute-done.3), channel_id=1, source_target_pairs={{0,15},{1,0},{2,1},{3,2},{4,3},{5,4},{6,5},{7,6},{8,7},{9,8},{10,9... | collective-permute-start | bytes 245768 | tf_op jit(solution)/shard_map/ppermute | solution.py:33
  35.2 7.5 %collective-permute-start.6 = (bf16[10,64,64]{2,1,0:T(8,128)(2,1)S(1)}, bf16[10,64,64]{2,1,0:T(8,128)(2,1)S(1)}, u32[]{:S(2)}, u32[]{:S(2)}) collective-permute-start(bf16[10,64,64]{2,1,0:T(8,128)(2,1)S(1)} %collective-permute-done.4), channel_id=1, source_target_pairs={{0,1},{1,2},{2,3},{3,4},{4,5},{5,6},{6,7},{7,8},{8,9},{9,10},{10,1... | collective-permute-start | bytes 245768 | tf_op jit(solution)/shard_map/ppermute | solution.py:26
  35.2 7.5 %collective-permute-start.7 = (bf16[10,64,64]{2,1,0:T(8,128)(2,1)S(1)}, bf16[10,64,64]{2,1,0:T(8,128)(2,1)S(1)}, u32[]{:S(2)}, u32[]{:S(2)}) collective-permute-start(bf16[10,64,64]{2,1,0:T(8,128)(2,1)S(1)} %collective-permute-done.5), channel_id=1, source_target_pairs={{0,15},{1,0},{2,1},{3,2},{4,3},{5,4},{6,5},{7,6},{8,7},{9,8},{10,9... | collective-permute-start | bytes 245768 | tf_op jit(solution)/shard_map/ppermute | solution.py:33
  39.6 34.8 %copy-start.3 = (f32[1024,64]{0,1:T(8,128)S(1)}, f32[1024,64]{0,1:T(8,128)}, u32[]{:S(2)}) copy-start(f32[1024,64]{0,1:T(8,128)} %param.5) | copy-start | bytes 786436
  42.7 7.5 %collective-permute-start.8 = (bf16[10,64,64]{2,1,0:T(8,128)(2,1)S(1)}, bf16[10,64,64]{2,1,0:T(8,128)(2,1)S(1)}, u32[]{:S(2)}, u32[]{:S(2)}) collective-permute-start(bf16[10,64,64]{2,1,0:T(8,128)(2,1)S(1)} %collective-permute-done.6), channel_id=1, source_target_pairs={{0,1},{1,2},{2,3},{3,4},{4,5},{5,6},{6,7},{7,8},{8,9},{9,10},{10,1... | collective-permute-start | bytes 245768 | tf_op jit(solution)/shard_map/ppermute | solution.py:26
  42.7 7.5 %collective-permute-start.9 = (bf16[10,64,64]{2,1,0:T(8,128)(2,1)S(1)}, bf16[10,64,64]{2,1,0:T(8,128)(2,1)S(1)}, u32[]{:S(2)}, u32[]{:S(2)}) collective-permute-start(bf16[10,64,64]{2,1,0:T(8,128)(2,1)S(1)} %collective-permute-done.7), channel_id=1, source_target_pairs={{0,15},{1,0},{2,1},{3,2},{4,3},{5,4},{6,5},{7,6},{8,7},{9,8},{10,9... | collective-permute-start | bytes 245768 | tf_op jit(solution)/shard_map/ppermute | solution.py:33
  50.3 7.5 %collective-permute-start.10 = (bf16[10,64,64]{2,1,0:T(8,128)(2,1)S(1)}, bf16[10,64,64]{2,1,0:T(8,128)(2,1)S(1)}, u32[]{:S(2)}, u32[]{:S(2)}) collective-permute-start(bf16[10,64,64]{2,1,0:T(8,128)(2,1)S(1)} %collective-permute-done.8), channel_id=1, source_target_pairs={{0,1},{1,2},{2,3},{3,4},{4,5},{5,6},{6,7},{7,8},{8,9},{9,10},{10,1... | collective-permute-start | bytes 245768 | tf_op jit(solution)/shard_map/ppermute | solution.py:26
  50.3 7.5 %collective-permute-start.11 = (bf16[10,64,64]{2,1,0:T(8,128)(2,1)S(1)}, bf16[10,64,64]{2,1,0:T(8,128)(2,1)S(1)}, u32[]{:S(2)}, u32[]{:S(2)}) collective-permute-start(bf16[10,64,64]{2,1,0:T(8,128)(2,1)S(1)} %collective-permute-done.9), channel_id=1, source_target_pairs={{0,15},{1,0},{2,1},{3,2},{4,3},{5,4},{6,5},{7,6},{8,7},{9,8},{10,9... | collective-permute-start | bytes 245768 | tf_op jit(solution)/shard_map/ppermute | solution.py:33
  57.8 7.4 %collective-permute-start.12 = (bf16[10,64,64]{2,1,0:T(8,128)(2,1)S(1)}, bf16[10,64,64]{2,1,0:T(8,128)(2,1)S(1)}, u32[]{:S(2)}, u32[]{:S(2)}) collective-permute-start(bf16[10,64,64]{2,1,0:T(8,128)(2,1)S(1)} %collective-permute-done.10), channel_id=1, source_target_pairs={{0,1},{1,2},{2,3},{3,4},{4,5},{5,6},{6,7},{7,8},{8,9},{9,10},{10,1... | collective-permute-start | bytes 245768 | tf_op jit(solution)/shard_map/ppermute | solution.py:26
  57.8 7.5 %collective-permute-start.13 = (bf16[10,64,64]{2,1,0:T(8,128)(2,1)S(1)}, bf16[10,64,64]{2,1,0:T(8,128)(2,1)S(1)}, u32[]{:S(2)}, u32[]{:S(2)}) collective-permute-start(bf16[10,64,64]{2,1,0:T(8,128)(2,1)S(1)} %collective-permute-done.11), channel_id=1, source_target_pairs={{0,15},{1,0},{2,1},{3,2},{4,3},{5,4},{6,5},{7,6},{8,7},{9,8},{10,9... | collective-permute-start | bytes 245768 | tf_op jit(solution)/shard_map/ppermute | solution.py:33
  65.3 7.4 %collective-permute-start.14 = (bf16[10,64,64]{2,1,0:T(8,128)(2,1)S(1)}, bf16[10,64,64]{2,1,0:T(8,128)(2,1)S(1)}, u32[]{:S(2)}, u32[]{:S(2)}) collective-permute-start(bf16[10,64,64]{2,1,0:T(8,128)(2,1)S(1)} %collective-permute-done.12), channel_id=1, source_target_pairs={{0,1},{1,2},{2,3},{3,4},{4,5},{5,6},{6,7},{7,8},{8,9},{9,10},{10,1... | collective-permute-start | bytes 245768 | tf_op jit(solution)/shard_map/ppermute | solution.py:26
  95.8 18.0 %all-to-all-start = ((bf16[16,2,8192]{2,1,0:T(2,128)(2,1)}), bf16[16,2,8192]{2,1,0:T(2,128)(2,1)S(1)}, u32[]{:S(2)}, u32[]{:S(2)}) async-start(bf16[16,2,8192]{2,1,0:T(2,128)(2,1)} %reshape.84), calls=%async_computation | async-start | bytes 1048576 | tf_op jit(solution)/shard_map/all_to_all | solution.py:88
  115.3 7.5 %collective-permute-start.15 = (bf16[10,64,64]{2,1,0:T(8,128)(2,1)S(1)}, bf16[10,64,64]{2,1,0:T(8,128)(2,1)S(1)}, u32[]{:S(2)}, u32[]{:S(2)}) collective-permute-start(bf16[10,64,64]{2,1,0:T(8,128)(2,1)S(1)} %bitcast.65), channel_id=1, source_target_pairs={{0,1},{1,2},{2,3},{3,4},{4,5},{5,6},{6,7},{7,8},{8,9},{9,10},{10,1... | collective-permute-start | bytes 245768 | tf_op jit(solution)/shard_map/ppermute | solution.py:26
  115.4 7.5 %collective-permute-start.16 = (bf16[10,64,64]{2,1,0:T(8,128)(2,1)S(1)}, bf16[10,64,64]{2,1,0:T(8,128)(2,1)S(1)}, u32[]{:S(2)}, u32[]{:S(2)}) collective-permute-start(bf16[10,64,64]{2,1,0:T(8,128)(2,1)S(1)} %bitcast.66), channel_id=1, source_target_pairs={{0,15},{1,0},{2,1},{3,2},{4,3},{5,4},{6,5},{7,6},{8,7},{9,8},{10,9... | collective-permute-start | bytes 245768 | tf_op jit(solution)/shard_map/ppermute | solution.py:33
  122.8 7.5 %collective-permute-start.17 = (bf16[10,64,64]{2,1,0:T(8,128)(2,1)S(1)}, bf16[10,64,64]{2,1,0:T(8,128)(2,1)S(1)}, u32[]{:S(2)}, u32[]{:S(2)}) collective-permute-start(bf16[10,64,64]{2,1,0:T(8,128)(2,1)S(1)} %collective-permute-done.15), channel_id=1, source_target_pairs={{0,1},{1,2},{2,3},{3,4},{4,5},{5,6},{6,7},{7,8},{8,9},{9,10},{10,1... | collective-permute-start | bytes 245768 | tf_op jit(solution)/shard_map/ppermute | solution.py:26
  122.9 7.5 %collective-permute-start.18 = (bf16[10,64,64]{2,1,0:T(8,128)(2,1)S(1)}, bf16[10,64,64]{2,1,0:T(8,128)(2,1)S(1)}, u32[]{:S(2)}, u32[]{:S(2)}) collective-permute-start(bf16[10,64,64]{2,1,0:T(8,128)(2,1)S(1)} %collective-permute-done.16), channel_id=1, source_target_pairs={{0,15},{1,0},{2,1},{3,2},{4,3},{5,4},{6,5},{7,6},{8,7},{9,8},{10,9... | collective-permute-start | bytes 245768 | tf_op jit(solution)/shard_map/ppermute | solution.py:33
  130.4 7.5 %collective-permute-start.19 = (bf16[10,64,64]{2,1,0:T(8,128)(2,1)S(1)}, bf16[10,64,64]{2,1,0:T(8,128)(2,1)S(1)}, u32[]{:S(2)}, u32[]{:S(2)}) collective-permute-start(bf16[10,64,64]{2,1,0:T(8,128)(2,1)S(1)} %collective-permute-done.17), channel_id=1, source_target_pairs={{0,1},{1,2},{2,3},{3,4},{4,5},{5,6},{6,7},{7,8},{8,9},{9,10},{10,1... | collective-permute-start | bytes 245768 | tf_op jit(solution)/shard_map/ppermute | solution.py:26
  130.4 7.5 %collective-permute-start.20 = (bf16[10,64,64]{2,1,0:T(8,128)(2,1)S(1)}, bf16[10,64,64]{2,1,0:T(8,128)(2,1)S(1)}, u32[]{:S(2)}, u32[]{:S(2)}) collective-permute-start(bf16[10,64,64]{2,1,0:T(8,128)(2,1)S(1)} %collective-permute-done.18), channel_id=1, source_target_pairs={{0,15},{1,0},{2,1},{3,2},{4,3},{5,4},{6,5},{7,6},{8,7},{9,8},{10,9... | collective-permute-start | bytes 245768 | tf_op jit(solution)/shard_map/ppermute | solution.py:33
  137.9 7.5 %collective-permute-start.21 = (bf16[10,64,64]{2,1,0:T(8,128)(2,1)S(1)}, bf16[10,64,64]{2,1,0:T(8,128)(2,1)S(1)}, u32[]{:S(2)}, u32[]{:S(2)}) collective-permute-start(bf16[10,64,64]{2,1,0:T(8,128)(2,1)S(1)} %collective-permute-done.19), channel_id=1, source_target_pairs={{0,1},{1,2},{2,3},{3,4},{4,5},{5,6},{6,7},{7,8},{8,9},{9,10},{10,1... | collective-permute-start | bytes 245768 | tf_op jit(solution)/shard_map/ppermute | solution.py:26
  137.9 7.5 %collective-permute-start.22 = (bf16[10,64,64]{2,1,0:T(8,128)(2,1)S(1)}, bf16[10,64,64]{2,1,0:T(8,128)(2,1)S(1)}, u32[]{:S(2)}, u32[]{:S(2)}) collective-permute-start(bf16[10,64,64]{2,1,0:T(8,128)(2,1)S(1)} %collective-permute-done.20), channel_id=1, source_target_pairs={{0,15},{1,0},{2,1},{3,2},{4,3},{5,4},{6,5},{7,6},{8,7},{9,8},{10,9... | collective-permute-start | bytes 245768 | tf_op jit(solution)/shard_map/ppermute | solution.py:33
  145.5 7.5 %collective-permute-start.23 = (bf16[10,64,64]{2,1,0:T(8,128)(2,1)S(1)}, bf16[10,64,64]{2,1,0:T(8,128)(2,1)S(1)}, u32[]{:S(2)}, u32[]{:S(2)}) collective-permute-start(bf16[10,64,64]{2,1,0:T(8,128)(2,1)S(1)} %collective-permute-done.21), channel_id=1, source_target_pairs={{0,1},{1,2},{2,3},{3,4},{4,5},{5,6},{6,7},{7,8},{8,9},{9,10},{10,1... | collective-permute-start | bytes 245768 | tf_op jit(solution)/shard_map/ppermute | solution.py:26
  145.5 7.5 %collective-permute-start.24 = (bf16[10,64,64]{2,1,0:T(8,128)(2,1)S(1)}, bf16[10,64,64]{2,1,0:T(8,128)(2,1)S(1)}, u32[]{:S(2)}, u32[]{:S(2)}) collective-permute-start(bf16[10,64,64]{2,1,0:T(8,128)(2,1)S(1)} %collective-permute-done.22), channel_id=1, source_target_pairs={{0,15},{1,0},{2,1},{3,2},{4,3},{5,4},{6,5},{7,6},{8,7},{9,8},{10,9... | collective-permute-start | bytes 245768 | tf_op jit(solution)/shard_map/ppermute | solution.py:33
  153.0 7.5 %collective-permute-start.25 = (bf16[10,64,64]{2,1,0:T(8,128)(2,1)S(1)}, bf16[10,64,64]{2,1,0:T(8,128)(2,1)S(1)}, u32[]{:S(2)}, u32[]{:S(2)}) collective-permute-start(bf16[10,64,64]{2,1,0:T(8,128)(2,1)S(1)} %collective-permute-done.23), channel_id=1, source_target_pairs={{0,1},{1,2},{2,3},{3,4},{4,5},{5,6},{6,7},{7,8},{8,9},{9,10},{10,1... | collective-permute-start | bytes 245768 | tf_op jit(solution)/shard_map/ppermute | solution.py:26
  153.0 7.5 %collective-permute-start.26 = (bf16[10,64,64]{2,1,0:T(8,128)(2,1)S(1)}, bf16[10,64,64]{2,1,0:T(8,128)(2,1)S(1)}, u32[]{:S(2)}, u32[]{:S(2)}) collective-permute-start(bf16[10,64,64]{2,1,0:T(8,128)(2,1)S(1)} %collective-permute-done.24), channel_id=1, source_target_pairs={{0,15},{1,0},{2,1},{3,2},{4,3},{5,4},{6,5},{7,6},{8,7},{9,8},{10,9... | collective-permute-start | bytes 245768 | tf_op jit(solution)/shard_map/ppermute | solution.py:33
  160.6 7.4 %collective-permute-start.27 = (bf16[10,64,64]{2,1,0:T(8,128)(2,1)S(1)}, bf16[10,64,64]{2,1,0:T(8,128)(2,1)S(1)}, u32[]{:S(2)}, u32[]{:S(2)}) collective-permute-start(bf16[10,64,64]{2,1,0:T(8,128)(2,1)S(1)} %collective-permute-done.25), channel_id=1, source_target_pairs={{0,1},{1,2},{2,3},{3,4},{4,5},{5,6},{6,7},{7,8},{8,9},{9,10},{10,1... | collective-permute-start | bytes 245768 | tf_op jit(solution)/shard_map/ppermute | solution.py:26
  160.6 7.4 %collective-permute-start.28 = (bf16[10,64,64]{2,1,0:T(8,128)(2,1)S(1)}, bf16[10,64,64]{2,1,0:T(8,128)(2,1)S(1)}, u32[]{:S(2)}, u32[]{:S(2)}) collective-permute-start(bf16[10,64,64]{2,1,0:T(8,128)(2,1)S(1)} %collective-permute-done.26), channel_id=1, source_target_pairs={{0,15},{1,0},{2,1},{3,2},{4,3},{5,4},{6,5},{7,6},{8,7},{9,8},{10,9... | collective-permute-start | bytes 245768 | tf_op jit(solution)/shard_map/ppermute | solution.py:33
  168.0 7.4 %collective-permute-start.29 = (bf16[10,64,64]{2,1,0:T(8,128)(2,1)S(1)}, bf16[10,64,64]{2,1,0:T(8,128)(2,1)S(1)}, u32[]{:S(2)}, u32[]{:S(2)}) collective-permute-start(bf16[10,64,64]{2,1,0:T(8,128)(2,1)S(1)} %collective-permute-done.27), channel_id=1, source_target_pairs={{0,1},{1,2},{2,3},{3,4},{4,5},{5,6},{6,7},{7,8},{8,9},{9,10},{10,1... | collective-permute-start | bytes 245768 | tf_op jit(solution)/shard_map/ppermute | solution.py:26
  (5 other events, 26.5 us)
